TPU v7x, 128 devices: a whole 4x4x4 slice. The times are simulated.
128 devices in a mesh: row: 8 (over y_lo, z), col: 16 (over x, y_hi, core).
Axes of the slice: x: 4, y: 4 (y_hi: 2, y_lo: 2; y = y_hi * 2 + y_lo), z: 4, core: 2. Of those that a mesh axis runs over, the one named last changes fastest.
Arguments:
- x_blocks: bfloat16 [2048, 2048, 128], P('row', 'col'), may hold values from -0.046875 to 0.046875
- block_ids: int32 [2048, 16], P('row', 'col'), may hold values from 0 to 511, as said below
- margins: float32 [32768], P('row'), may hold values from -6 to 6
- deleted: int32 [4096], P('row'), may hold values from 0 to 32767, as said below
- grads: float32 [32768, 128], P('col'), may hold values from -6 to 6
Outputs:
- solution: float32 [32768, 128], P('col')
- residual: float32 [32768, 128], P('col')
Inputs may be any that keep to these rules, and one draw needn't show every extreme that they name: `block_ids`: each device's 256 entries are distinct and rise; each device lists the first and the last block of its grid. `deleted`: the 512 entries of row shard r are distinct rows of that shard, r * 4096 and up; each shard deletes its first and its last row.
All inputs are finite; a program needn't handle non-finite values.
Results may differ from a plain program's by a relative error of at most 0.015.
Values may be sent and summed in bfloat16 or wider, within the bound.
A program may use at most 128 MiB of HBM per device.

v0:
```python
import jax
import jax.numpy as jnp
from jax import lax
from jax.sharding import Mesh
from jax.sharding import PartitionSpec as P

ITERS = 3
ROW = ("row_0", "row_1")
COL = ("col_0", "col_1", "col_2")
ROW_COL = ("row_0", "row_1", "col_0", "col_1", "col_2")
highest = lax.Precision.HIGHEST
ridge_weight = 0.2


def cut_along(shard, dim, size):
    before, after = (shard.shape[:dim], shard.shape[dim + 1 :])
    return jnp.moveaxis(shard.reshape(*before, size, -1, *after), dim, 0)


def sent_and_summed(shard, axis, dim):
    pieces = cut_along(shard, dim, lax.axis_size(axis))
    arrived = lax.all_to_all(pieces, axis, split_axis=0, concat_axis=0, tiled=True)
    return arrived.sum(axis=0)


def from_everyone(shard, axis):
    size = lax.axis_size(axis)
    return lax.all_to_all(
        jnp.broadcast_to(shard[None], (size, *shard.shape)), axis, 0, 0, tiled=True
    )


def laid_out(pieces, dim):
    shape = list(pieces.shape[1:])
    shape[dim] *= pieces.shape[0]
    return jnp.moveaxis(pieces, 0, dim).reshape(shape)


def gather_directly(shard, axis, dim):
    pieces = from_everyone(shard, axis)
    return laid_out(pieces, dim)


def by_axis(shard, axes):
    for axis in axes:
        shard = lax.psum(shard, axis)
    return shard


def in_one_piece(arrays, axis, dim, along):
    both = jnp.concatenate(arrays, axis=along)
    result, at, outs = (lax.all_gather(both, axis, axis=dim, tiled=True), 0, [])
    for a in arrays:
        outs.append(lax.slice_in_dim(result, at, at + a.shape[along], axis=along))
        at += a.shape[along]
    return tuple(outs)


def on_device(x_blocks, block_ids, margins, deleted, grads):
    block_width = x_blocks.shape[1]
    feature_rows = grads.shape[0]
    directions = grads.shape[1]
    row_count = margins.shape[0]
    row_blocks = row_count // block_width
    feature_blocks = feature_rows // block_width
    pattern = block_ids[:, 0]
    block_row = pattern // feature_blocks
    block_column = pattern % feature_blocks
    row_select = (block_row[:, None] == jnp.arange(row_blocks, dtype=jnp.int32)[None, :]).astype(
        jnp.float32
    )
    column_select = (
        block_column[:, None] == jnp.arange(feature_blocks, dtype=jnp.int32)[None, :]
    ).astype(jnp.float32)
    global_rows = lax.axis_index(ROW) * row_count + jnp.arange(row_count, dtype=jnp.int32)
    removed = jnp.any(global_rows[:, None] == deleted[None, :], axis=1)
    logistic = jax.nn.sigmoid(margins)
    weights_flat = jnp.where(removed, 0.0, logistic * (1.0 - logistic))
    row_share_count = row_count // lax.axis_size(COL)
    row_offset = lax.axis_index(COL) * row_share_count
    share_rows = feature_rows // lax.axis_size(ROW)
    offset = lax.axis_index(ROW) * share_rows
    residual = lax.dynamic_slice_in_dim(grads, offset, share_rows, 0)
    solution = jnp.zeros_like(residual)
    direction = residual
    mine = residual
    norm_now = by_axis(jnp.sum(mine * mine, axis=0), ROW_COL)
    for iteration in range(ITERS):
        apply_rounded = direction.astype(jnp.bfloat16)
        gathered = gather_directly(apply_rounded, ROW, 0)
        picked_tiles = gathered.reshape(feature_blocks, block_width, directions)[block_column]
        forward = jnp.einsum(
            "bij,bjk->bik", x_blocks, picked_tiles, preferred_element_type=jnp.float32
        )
        partial_rows = jnp.einsum("br,bik->rik", row_select, forward, precision=highest)
        flat_rows = partial_rows.reshape(row_count, directions)
        own_sum = sent_and_summed(flat_rows, COL, 0)
        own_weights = lax.dynamic_slice_in_dim(weights_flat, row_offset, row_share_count, 0)
        own_scaled = (own_weights[:, None] * own_sum).astype(jnp.bfloat16)
        scaled = gather_directly(own_scaled, COL, 0).reshape(row_blocks, block_width, directions)
        picked_rows = scaled[block_row]
        backward = jnp.einsum(
            "bji,bjk->bik", x_blocks, picked_rows, preferred_element_type=jnp.float32
        )
        summed = jnp.einsum("bc,bik->cik", column_select, backward, precision=highest)
        hessian_image = (
            sent_and_summed(summed.reshape(feature_rows, directions), ROW, 0)
            + ridge_weight * direction
        )
        own_residual = residual
        curvature, cross_term, image_square = (
            by_axis(jnp.sum(direction * hessian_image, axis=0), ROW_COL),
            by_axis(jnp.sum(own_residual * hessian_image, axis=0), ROW_COL),
            by_axis(jnp.sum(hessian_image * hessian_image, axis=0), ROW_COL),
        )
        step_size = norm_now / curvature
        norm_next = norm_now - 2.0 * step_size * cross_term + step_size * step_size * image_square
        solution = solution + step_size * direction
        residual = residual - step_size * hessian_image
        if iteration + 1 < ITERS:
            direction = residual + norm_next / norm_now * direction
            norm_now = norm_next
    solution, residual = tuple(
        (
            part.astype(jnp.float32)
            for part in in_one_piece(
                (solution.astype(jnp.bfloat16), residual.astype(jnp.bfloat16)), ROW, 0, 1
            )
        )
    )
    return (solution, residual)


def solution(mesh):
    torus = Mesh(mesh.devices.reshape(2, 4, 4, 2, 2), ("row_0", "row_1", "col_0", "col_1", "col_2"))
    in_specs = (P(ROW, COL, None), P(ROW, COL), P(ROW), P(ROW), P(COL, None))
    out_specs = (P(COL, None), P(COL, None))
    return jax.shard_map(
        on_device, mesh=torus, in_specs=in_specs, out_specs=out_specs, check_vma=False
    )
```

profile of v0, /device:TPU:0, one launch (start us, length us, event | category | flops | bytes accessed | tf_op | source)
XLA Modules:
  0.0 715.4 jit_solution(13770284594476689411)
XLA Ops:
  9.0 6.4 all-to-all-start
  16.1 8.9 %all-to-all-done = bf16[8,256,128]{2,1,0:T(8,128)(2,1)S(1)} async-done(((bf16[8,256,128]{2,1,0:T(8,128)(2,1)}), bf16[8,256,128]{2,1,0:T(8,128)(2,1)S(1)}, u32[]{:S(2)}, u32[]{:S(2)}) %all-to-all-start) | async-done | bytes 524320 | tf_op jit(solution)/shard_map/all_to_all | solution.py:28
  24.9 8.6 %gather_fusion = bf16[256,128,128]{2,1,0:T(8,128)(2,1)} fusion(bf16[16,128,128]{2,1,0:T(8,128)(2,1)S(1)} %bitcast.56, s32[1024]{0:T(1024)S(1)} %pad_clamp_fusion.1), kind=kCustom, calls=%fused_computation | custom fusion | bytes 16778240 | tf_op jit(solution)/shard_map/gather | solution.py:91
  33.5 12.8 %convolution_bitcast_fusion.5 = f32[256,128,128]{1,2,0:T(8,128)} fusion(bf16[256,128,128]{2,1,0:T(8,128)(2,1)} %gather_fusion, bf16[256,128,128]{2,1,0:T(8,128)(2,1)} %param.5), kind=kOutput, calls=%fused_computation.11 | convolution fusion | flops 1073741824 | bytes 33554432 | tf_op jit(solution)/shard_map/bij,bjk->bik/dot_general | solution.py:92
  46.4 17.5 %copy.26 = f32[256,128,128]{2,0,1:T(8,128)} copy(f32[256,128,128]{1,2,0:T(8,128)} %convolution_bitcast_fusion.5) | data formatting | bytes 33554432 | tf_op jit(solution)/shard_map/bij,bjk->bik/dot_general | solution.py:92
  63.8 9.8 %fusion.5 = f32[32,128,128]{2,0,1:T(8,128)S(1)} fusion(f32[256,128,128]{2,0,1:T(8,128)} %copy.26, s32[256]{0:T(256)S(1)} %bitcast.71), kind=kOutput, calls=%fused_computation.40 | convolution fusion | flops 1610620928 | bytes 18875392 | tf_op jit(solution)/shard_map/br,bik->rik/dot_general | solution.py:95
  73.6 2.6 copy.27
  76.2 6.7 all-to-all-start.1
  83.0 1.5 compare_reduce_fusion
  84.6 27.5 %all-to-all-done.1 = f32[16,256,128]{2,1,0:T(8,128)S(1)} async-done(((f32[16,256,128]{2,1,0:T(8,128)}), f32[16,256,128]{2,1,0:T(8,128)S(1)}, u32[]{:S(2)}, u32[]{:S(2)}) %all-to-all-start.1) | async-done | bytes 2097184 | tf_op jit(solution)/shard_map/all_to_all | solution.py:22
  112.4 1.2 broadcast_in_dim.18
  113.5 4.9 all-to-all-start.2
  118.7 17.7 %all-to-all-done.2 = bf16[16,256,128]{2,1,0:T(8,128)(2,1)S(1)} async-done(((bf16[16,256,128]{2,1,0:T(8,128)(2,1)}), bf16[16,256,128]{2,1,0:T(8,128)(2,1)S(1)}, u32[]{:S(2)}, u32[]{:S(2)}) %all-to-all-start.2) | async-done | bytes 1048608 | tf_op jit(solution)/shard_map/all_to_all | solution.py:28
  136.4 8.6 %gather_fusion.1 = bf16[256,128,128]{2,1,0:T(8,128)(2,1)} fusion(bf16[32,128,128]{2,1,0:T(8,128)(2,1)S(1)} %bitcast.59, s32[1024]{0:T(1024)S(1)} %pad_clamp_fusion), kind=kCustom, calls=%fused_computation.1 | custom fusion | bytes 16778240 | tf_op jit(solution)/shard_map/gather | solution.py:101
  145.0 14.4 %convolution_bitcast_fusion.4 = f32[256,128,128]{1,2,0:T(8,128)} fusion(bf16[256,128,128]{2,1,0:T(8,128)(2,1)} %gather_fusion.1, bf16[256,128,128]{2,1,0:T(8,128)(2,1)} %param.5), kind=kOutput, calls=%fused_computation.10 | convolution fusion | flops 1073741824 | bytes 33554432 | tf_op jit(solution)/shard_map/bji,bjk->bik/dot_general | solution.py:102
  159.4 17.5 %copy.29 = f32[256,128,128]{2,0,1:T(8,128)} copy(f32[256,128,128]{1,2,0:T(8,128)} %convolution_bitcast_fusion.4) | data formatting | bytes 33554432 | tf_op jit(solution)/shard_map/bji,bjk->bik/dot_general | solution.py:102
  176.9 9.0 %fusion.15 = f32[16,128,128]{2,0,1:T(8,128)S(1)} fusion(f32[256,128,128]{2,0,1:T(8,128)} %copy.29, s32[256]{0:T(256)S(1)} %bitcast.68), kind=kOutput, calls=%fused_computation.49 | convolution fusion | flops 805310464 | bytes 17826816 | tf_op jit(solution)/shard_map/bc,bik->cik/dot_general | solution.py:105
  186.3 18.3 %all_to_all.60 = f32[8,256,128]{2,1,0:T(8,128)S(1)} all-to-all(f32[8,256,128]{2,1,0:T(8,128)S(1)} %bitcast.65), channel_id=1, replica_groups=mesh['row_0'=2,'row_1'=4,'col_0'=4,'col_1'=2,'col_2'=2] {'row_0','row_1'}, dimensions={0} | all-to-all | bytes 2097152 | tf_op jit(solution)/shard_map/all_to_all | solution.py:22
  204.6 1.0 multiply_reduce_fusion.4
  205.6 4.9 all-reduce.9
  210.5 8.5 %all-reduce.3 = (f32[128]{0:T(128)S(1)}, f32[128]{0:T(128)S(1)}, f32[128]{0:T(128)S(1)}) all-reduce(f32[128]{0:T(128)S(1)} %get-tuple-element.35, f32[128]{0:T(128)S(1)} %get-tuple-element.36, f32[128]{0:T(128)S(1)} %get-tuple-element.37), channel_id=1, replica_groups=mesh['row_0'=2,'row_1'=4,'col_0'=4,'col_1'=2,'col_2'=2] {'row_1'}, use_global_device_ids=true, to_apply=%region_2.3 | all-reduce | flops 384 | bytes 3072 | tf_op jit(solution)/shard_map/psum | solution.py:46
  219.0 8.7 %all-reduce.1 = (f32[128]{0:T(128)S(1)}, f32[128]{0:T(128)S(1)}, f32[128]{0:T(128)S(1)}) all-reduce(f32[128]{0:T(128)S(1)} %get-tuple-element.17, f32[128]{0:T(128)S(1)} %get-tuple-element.18, f32[128]{0:T(128)S(1)} %get-tuple-element.19), channel_id=1, replica_groups=mesh['row_0'=2,'row_1'=4,'col_0'=4,'col_1'=2,'col_2'=2] {'col_0'}, use_global_device_ids=true, to_apply=%region_3.4 | all-reduce | flops 384 | bytes 3072 | tf_op jit(solution)/shard_map/psum | solution.py:46
  227.7 6.4 all-reduce.7
  234.1 2.4 all-reduce.5
  236.6 0.9 fusion.24
  237.6 13.4 %all_to_all.61 = bf16[8,256,128]{2,1,0:T(8,128)(2,1)S(1)} all-to-all(bf16[8,256,128]{2,1,0:T(8,128)(2,1)S(1)} %broadcast_in_dim.19), channel_id=1, replica_groups=mesh['row_0'=2,'row_1'=4,'col_0'=4,'col_1'=2,'col_2'=2] {'row_0','row_1'}, dimensions={0} | all-to-all | bytes 1048576 | tf_op jit(solution)/shard_map/all_to_all | solution.py:28
  251.0 8.6 %gather_fusion.2 = bf16[256,128,128]{2,1,0:T(8,128)(2,1)} fusion(bf16[16,128,128]{2,1,0:T(8,128)(2,1)S(1)} %bitcast.58, s32[1024]{0:T(1024)S(1)} %pad_clamp_fusion.1), kind=kCustom, calls=%fused_computation.2 | custom fusion | bytes 16778240 | tf_op jit(solution)/shard_map/gather | solution.py:91
  259.6 12.8 %convolution_bitcast_fusion.3 = f32[256,128,128]{1,2,0:T(8,128)} fusion(bf16[256,128,128]{2,1,0:T(8,128)(2,1)} %gather_fusion.2, bf16[256,128,128]{2,1,0:T(8,128)(2,1)} %param.5), kind=kOutput, calls=%fused_computation.9 | convolution fusion | flops 1073741824 | bytes 33554432 | tf_op jit(solution)/shard_map/bij,bjk->bik/dot_general | solution.py:92
  272.4 17.5 %copy.32 = f32[256,128,128]{2,0,1:T(8,128)} copy(f32[256,128,128]{1,2,0:T(8,128)} %convolution_bitcast_fusion.3) | data formatting | bytes 33554432 | tf_op jit(solution)/shard_map/bij,bjk->bik/dot_general | solution.py:92
  289.9 9.8 %fusion.3 = f32[32,128,128]{2,0,1:T(8,128)S(1)} fusion(f32[256,128,128]{2,0,1:T(8,128)} %copy.32, s32[256]{0:T(256)S(1)} %bitcast.72), kind=kOutput, calls=%fused_computation.39 | convolution fusion | flops 1610620928 | bytes 18875392 | tf_op jit(solution)/shard_map/br,bik->rik/dot_general | solution.py:95
  299.7 1.2 copy.33
  300.9 32.3 %all_to_all.62 = f32[16,256,128]{2,1,0:T(8,128)S(1)} all-to-all(f32[16,256,128]{2,1,0:T(8,128)S(1)} %bitcast.63), channel_id=1, replica_groups=mesh['row_0'=2,'row_1'=4,'col_0'=4,'col_1'=2,'col_2'=2] {'col_0','col_1'..., dimensions={0} | all-to-all | bytes 4194304 | tf_op jit(solution)/shard_map/all_to_all | solution.py:22
  333.6 20.8 %all_to_all.63 = bf16[16,256,128]{2,1,0:T(8,128)(2,1)S(1)} all-to-all(bf16[16,256,128]{2,1,0:T(8,128)(2,1)S(1)} %broadcast_in_dim.20), channel_id=1, replica_groups=mesh['row_0'=2,'row_1'=4,'col_0'=4,'col_1'=2,'col_2'=2] {'col_0','col_1'..., dimensions={0} | all-to-all | bytes 2097152 | tf_op jit(solution)/shard_map/all_to_all | solution.py:28
  354.4 8.6 %gather_fusion.3 = bf16[256,128,128]{2,1,0:T(8,128)(2,1)} fusion(bf16[32,128,128]{2,1,0:T(8,128)(2,1)S(1)} %bitcast.61, s32[1024]{0:T(1024)S(1)} %pad_clamp_fusion), kind=kCustom, calls=%fused_computation.3 | custom fusion | bytes 16778240 | tf_op jit(solution)/shard_map/gather | solution.py:101
  363.0 14.4 %convolution_bitcast_fusion.2 = f32[256,128,128]{1,2,0:T(8,128)} fusion(bf16[256,128,128]{2,1,0:T(8,128)(2,1)} %gather_fusion.3, bf16[256,128,128]{2,1,0:T(8,128)(2,1)} %param.5), kind=kOutput, calls=%fused_computation.8 | convolution fusion | flops 1073741824 | bytes 33554432 | tf_op jit(solution)/shard_map/bji,bjk->bik/dot_general | solution.py:102
  377.4 17.5 %copy.35 = f32[256,128,128]{2,0,1:T(8,128)} copy(f32[256,128,128]{1,2,0:T(8,128)} %convolution_bitcast_fusion.2) | data formatting | bytes 33554432 | tf_op jit(solution)/shard_map/bji,bjk->bik/dot_general | solution.py:102
  394.8 9.0 %fusion.13 = f32[16,128,128]{2,0,1:T(8,128)S(1)} fusion(f32[256,128,128]{2,0,1:T(8,128)} %copy.35, s32[256]{0:T(256)S(1)} %bitcast.69), kind=kOutput, calls=%fused_computation.48 | convolution fusion | flops 805310464 | bytes 17826816 | tf_op jit(solution)/shard_map/bc,bik->cik/dot_general | solution.py:105
  404.2 17.7 %all_to_all.64 = f32[8,256,128]{2,1,0:T(8,128)S(1)} all-to-all(f32[8,256,128]{2,1,0:T(8,128)S(1)} %bitcast.66), channel_id=1, replica_groups=mesh['row_0'=2,'row_1'=4,'col_0'=4,'col_1'=2,'col_2'=2] {'row_0','row_1'}, dimensions={0} | all-to-all | bytes 2097152 | tf_op jit(solution)/shard_map/all_to_all | solution.py:22
  422.0 4.9 all-reduce.8
  427.0 8.5 %all-reduce.2 = (f32[128]{0:T(128)S(1)}, f32[128]{0:T(128)S(1)}, f32[128]{0:T(128)S(1)}) all-reduce(f32[128]{0:T(128)S(1)} %get-tuple-element.32, f32[128]{0:T(128)S(1)} %get-tuple-element.33, f32[128]{0:T(128)S(1)} %get-tuple-element.34), channel_id=1, replica_groups=mesh['row_0'=2,'row_1'=4,'col_0'=4,'col_1'=2,'col_2'=2] {'row_1'}, use_global_device_ids=true, to_apply=%region_37.38 | all-reduce | flops 384 | bytes 3072 | tf_op jit(solution)/shard_map/psum | solution.py:46
  435.5 8.8 %all-reduce = (f32[128]{0:T(128)S(1)}, f32[128]{0:T(128)S(1)}, f32[128]{0:T(128)S(1)}) all-reduce(f32[128]{0:T(128)S(1)} %get-tuple-element.14, f32[128]{0:T(128)S(1)} %get-tuple-element.15, f32[128]{0:T(128)S(1)} %get-tuple-element.16), channel_id=1, replica_groups=mesh['row_0'=2,'row_1'=4,'col_0'=4,'col_1'=2,'col_2'=2] {'col_0'}, use_global_device_ids=true, to_apply=%region_38.39 | all-reduce | flops 384 | bytes 3072 | tf_op jit(solution)/shard_map/psum | solution.py:46
  444.3 6.4 all-reduce.6
  450.7 2.4 all-reduce.4
  453.3 13.2 %all_to_all.65 = bf16[8,256,128]{2,1,0:T(8,128)(2,1)S(1)} all-to-all(bf16[8,256,128]{2,1,0:T(8,128)(2,1)S(1)} %broadcast_in_dim.21), channel_id=1, replica_groups=mesh['row_0'=2,'row_1'=4,'col_0'=4,'col_1'=2,'col_2'=2] {'row_0','row_1'}, dimensions={0} | all-to-all | bytes 1048576 | tf_op jit(solution)/shard_map/all_to_all | solution.py:28
  466.5 8.6 %gather_fusion.4 = bf16[256,128,128]{2,1,0:T(8,128)(2,1)} fusion(bf16[16,128,128]{2,1,0:T(8,128)(2,1)S(1)} %bitcast.57, s32[1024]{0:T(1024)S(1)} %pad_clamp_fusion.1), kind=kCustom, calls=%fused_computation.4 | custom fusion | bytes 16778240 | tf_op jit(solution)/shard_map/gather | solution.py:91
  475.1 12.8 %convolution_bitcast_fusion.1 = f32[256,128,128]{1,2,0:T(8,128)} fusion(bf16[256,128,128]{2,1,0:T(8,128)(2,1)} %gather_fusion.4, bf16[256,128,128]{2,1,0:T(8,128)(2,1)} %param.5), kind=kOutput, calls=%fused_computation.7 | convolution fusion | flops 1073741824 | bytes 33554432 | tf_op jit(solution)/shard_map/bij,bjk->bik/dot_general | solution.py:92
  487.9 17.5 %copy.38 = f32[256,128,128]{2,0,1:T(8,128)} copy(f32[256,128,128]{1,2,0:T(8,128)} %convolution_bitcast_fusion.1) | data formatting | bytes 33554432 | tf_op jit(solution)/shard_map/bij,bjk->bik/dot_general | solution.py:92
  505.4 9.7 %fusion.1 = f32[32,128,128]{2,0,1:T(8,128)S(1)} fusion(f32[256,128,128]{2,0,1:T(8,128)} %copy.38, s32[256]{0:T(256)S(1)} %bitcast.73), kind=kOutput, calls=%fused_computation.38 | convolution fusion | flops 1610620928 | bytes 18875392 | tf_op jit(solution)/shard_map/br,bik->rik/dot_general | solution.py:95
  515.2 1.2 copy.39
  516.4 32.4 %all_to_all.66 = f32[16,256,128]{2,1,0:T(8,128)S(1)} all-to-all(f32[16,256,128]{2,1,0:T(8,128)S(1)} %bitcast.64), channel_id=1, replica_groups=mesh['row_0'=2,'row_1'=4,'col_0'=4,'col_1'=2,'col_2'=2] {'col_0','col_1'..., dimensions={0} | all-to-all | bytes 4194304 | tf_op jit(solution)/shard_map/all_to_all | solution.py:22
  549.2 20.8 %all_to_all.67 = bf16[16,256,128]{2,1,0:T(8,128)(2,1)S(1)} all-to-all(bf16[16,256,128]{2,1,0:T(8,128)(2,1)S(1)} %broadcast_in_dim.22), channel_id=1, replica_groups=mesh['row_0'=2,'row_1'=4,'col_0'=4,'col_1'=2,'col_2'=2] {'col_0','col_1'..., dimensions={0} | all-to-all | bytes 2097152 | tf_op jit(solution)/shard_map/all_to_all | solution.py:28
  570.0 8.6 %gather_fusion.5 = bf16[256,128,128]{2,1,0:T(8,128)(2,1)} fusion(bf16[32,128,128]{2,1,0:T(8,128)(2,1)S(1)} %bitcast.60, s32[1024]{0:T(1024)S(1)} %pad_clamp_fusion), kind=kCustom, calls=%fused_computation.5 | custom fusion | bytes 16778240 | tf_op jit(solution)/shard_map/gather | solution.py:101
  578.7 14.4 %convolution_bitcast_fusion = f32[256,128,128]{1,2,0:T(8,128)} fusion(bf16[256,128,128]{2,1,0:T(8,128)(2,1)} %gather_fusion.5, bf16[256,128,128]{2,1,0:T(8,128)(2,1)} %param.5), kind=kOutput, calls=%fused_computation.6 | convolution fusion | flops 1073741824 | bytes 33554432 | tf_op jit(solution)/shard_map/bji,bjk->bik/dot_general | solution.py:102
  593.0 17.5 %copy.41 = f32[256,128,128]{2,0,1:T(8,128)} copy(f32[256,128,128]{1,2,0:T(8,128)} %convolution_bitcast_fusion) | data formatting | bytes 33554432 | tf_op jit(solution)/shard_map/bji,bjk->bik/dot_general | solution.py:102
  610.5 9.0 %fusion.11 = f32[16,128,128]{2,0,1:T(8,128)S(1)} fusion(f32[256,128,128]{2,0,1:T(8,128)} %copy.41, s32[256]{0:T(256)S(1)} %bitcast.70), kind=kOutput, calls=%fused_computation.47 | convolution fusion | flops 805310464 | bytes 17826816 | tf_op jit(solution)/shard_map/bc,bik->cik/dot_general | solution.py:105
  619.9 17.7 %all_to_all.68 = f32[8,256,128]{2,1,0:T(8,128)S(1)} all-to-all(f32[8,256,128]{2,1,0:T(8,128)S(1)} %bitcast.67), channel_id=1, replica_groups=mesh['row_0'=2,'row_1'=4,'col_0'=4,'col_1'=2,'col_2'=2] {'row_0','row_1'}, dimensions={0} | all-to-all | bytes 2097152 | tf_op jit(solution)/shard_map/all_to_all | solution.py:22
  637.7 4.9 psum.290
  642.6 8.5 %psum.291 = f32[128]{0:T(128)S(1)} all-reduce(f32[128]{0:T(128)S(1)} %psum.290), channel_id=1, replica_groups=mesh['row_0'=2,'row_1'=4,'col_0'=4,'col_1'=2,'col_2'=2] {'row_1'}, use_global_device_ids=true, to_apply=%region_45.46 | all-reduce | flops 128 | bytes 1024 | tf_op jit(solution)/shard_map/psum | solution.py:46
  651.1 8.8 %psum.292 = f32[128]{0:T(128)S(1)} all-reduce(f32[128]{0:T(128)S(1)} %psum.291), channel_id=1, replica_groups=mesh['row_0'=2,'row_1'=4,'col_0'=4,'col_1'=2,'col_2'=2] {'col_0'}, use_global_device_ids=true, to_apply=%region_46.47 | all-reduce | flops 128 | bytes 1024 | tf_op jit(solution)/shard_map/psum | solution.py:46
  659.9 6.4 psum.293
  666.3 2.4 psum.294
  668.8 1.0 add_convert_fusion
  670.5 35.0 %all-gather.2.cloned.1.call-done = bf16[2048,256]{1,0:T(8,128)(2,1)} async-done(((bf16[256,256]{1,0:T(8,128)(2,1)}), bf16[2048,256]{1,0:T(8,128)(2,1)}) %all-gather.2.cloned.1.call-update) | async-done | bytes 1048592 | tf_op jit(solution)/shard_map/all_gather | solution.py:52
  705.5 2.7 slice_convert_fusion
  (38 shorter events, 6.0 us)
Async XLA Ops:
  9.0 16.0 %all-to-all-start = ((bf16[8,256,128]{2,1,0:T(8,128)(2,1)}), bf16[8,256,128]{2,1,0:T(8,128)(2,1)S(1)}, u32[]{:S(2)}, u32[]{:S(2)}) async-start(bf16[8,256,128]{2,1,0:T(8,128)(2,1)} %broadcast_in_dim.17), calls=%async_computation | async-start | bytes 1048576 | tf_op jit(solution)/shard_map/all_to_all | solution.py:28
  73.6 9.3 %copy-start = (f32[4096]{0:T(1024)S(1)}, f32[4096]{0:T(1024)}, u32[]{:S(2)}) copy-start(f32[4096]{0:T(1024)} %param.7) | copy-start | bytes 49156
  73.6 9.3 %copy-start.1 = (s32[512]{0:T(512)S(1)}, s32[512]{0:T(512)}, u32[]{:S(2)}) copy-start(s32[512]{0:T(512)} %param.8) | copy-start | bytes 6148
  76.2 36.0 %all-to-all-start.1 = ((f32[16,256,128]{2,1,0:T(8,128)}), f32[16,256,128]{2,1,0:T(8,128)S(1)}, u32[]{:S(2)}, u32[]{:S(2)}) async-start(f32[16,256,128]{2,1,0:T(8,128)} %bitcast.62), calls=%async_computation.1 | async-start | bytes 4194304 | tf_op jit(solution)/shard_map/all_to_all | solution.py:22
  113.5 22.9 %all-to-all-start.2 = ((bf16[16,256,128]{2,1,0:T(8,128)(2,1)}), bf16[16,256,128]{2,1,0:T(8,128)(2,1)S(1)}, u32[]{:S(2)}, u32[]{:S(2)}) async-start(bf16[16,256,128]{2,1,0:T(8,128)(2,1)} %broadcast_in_dim.18), calls=%async_computation.2 | async-start | bytes 2097152 | tf_op jit(solution)/shard_map/all_to_all | solution.py:28
  118.4 587.1 %all-gather.2.cloned.1.call-start = ((), (), s32[]{:S(2)}) async-start(), calls=%async_computation.12 | async-start | bytes 1179648 | tf_op jit(solution)/shard_map/all_gather | solution.py:52
Sparse Core Ops, SparseCore 0:
  670.6 34.8 all-gather.1
where the time goes:
time: 726 us; the launch traced here: 715 us
  blocking collectives  280 us (39%)
  local copies, waits for them, and re-layouts  166 us (23%)
  matrix products  138 us (19%)
  waiting for transfers between devices  89.2 us (12%)
  starting transfers between devices  18.2 us (3%)
  between operations  14.7 us (2%)
  other arithmetic  9.51 us (1%)
    all_to_all x5, blocking collectives, sent_and_summed(): lax.all_to_all(pieces, axis, split_axis=0, concat_axis=0, tiled=True)  118 us
    psum x15, blocking collectives, by_axis(): shard = lax.psum(shard, axis)  93.2 us
    all_to_all x4, blocking collectives, from_everyone(): lax.all_to_all(jnp.broadcast_to(shard[None], (size, *shard.shape)), axis,...  68.2 us
    dot_general x3, local copies, waits for them, and re-layouts, on_device(): jnp.einsum('bij,bjk->bik', x_blocks, picked_tiles, preferred_element_type...  52.4 us
    dot_general x3, local copies, waits for them, and re-layouts, on_device(): jnp.einsum('bji,bjk->bik', x_blocks, picked_rows, preferred_element_type=...  52.4 us
    dot_general x3, matrix products, on_device(): jnp.einsum('bji,bjk->bik', x_blocks, picked_rows, preferred_element_type=...  43.1 us
    dot_general x3, matrix products, on_device(): jnp.einsum('bij,bjk->bik', x_blocks, picked_tiles, preferred_element_type...  38.5 us
    all_gather x1, waiting for transfers between devices, in_one_piece(): result, at, outs = (lax.all_gather(both, axis, axis=dim, tiled=True), 0, [])  35 us
  transfers between devices with their start and end apart: 4, of which 4 were waited for; matrix products, arithmetic and copies ran while one was open for 0% of the time, Pallas kernels for 0%

commit v1 on v0

--- a/solution.py
+++ b/solution.py
@@ -43,7 +43,7 @@
 
 def by_axis(shard, axes):
     for axis in axes:
-        shard = lax.psum(shard, axis)
+        shard = jnp.sum(lax.all_gather(shard, axis), axis=0)
     return shard
 
 

time: 726 us -> 826 us (1.14)
  blocking collectives: 280 us -> 379 us
    all_gather x0 -> x35, blocking collectives: none -> 192 us  [by_axis(): shard = jnp.sum(lax.all_gather(shard, axis), axis=0)]
    psum x15 -> x0, blocking collectives: 93.2 us -> none  [by_axis(): shard = lax.psum(shard, axis)]
where the time goes in v1:
time: 826 us; the launch traced here: 815 us
  blocking collectives  379 us (46%)
  local copies, waits for them, and re-layouts  166 us (20%)
  matrix products  138 us (17%)
  waiting for transfers between devices  89.2 us (11%)
  starting transfers between devices  18.2 us (2%)
  between operations  14.8 us (2%)
  other arithmetic  10.2 us (1%)
    all_gather x35, blocking collectives, by_axis(): shard = jnp.sum(lax.all_gather(shard, axis), axis=0)  192 us
    all_to_all x5, blocking collectives, sent_and_summed(): lax.all_to_all(pieces, axis, split_axis=0, concat_axis=0, tiled=True)  118 us
    all_to_all x4, blocking collectives, from_everyone(): lax.all_to_all(jnp.broadcast_to(shard[None], (size, *shard.shape)), axis,...  68.3 us
    dot_general x3, local copies, waits for them, and re-layouts, on_device(): jnp.einsum('bij,bjk->bik', x_blocks, picked_tiles, preferred_element_type...  52.4 us
    dot_general x3, local copies, waits for them, and re-layouts, on_device(): jnp.einsum('bji,bjk->bik', x_blocks, picked_rows, preferred_element_type=...  52.4 us
    dot_general x3, matrix products, on_device(): jnp.einsum('bji,bjk->bik', x_blocks, picked_rows, preferred_element_type=...  43.1 us
    dot_general x3, matrix products, on_device(): jnp.einsum('bij,bjk->bik', x_blocks, picked_tiles, preferred_element_type...  38.5 us
    all_gather x1, waiting for transfers between devices, in_one_piece(): result, at, outs = (lax.all_gather(both, axis, axis=dim, tiled=True), 0, [])  35 us
  transfers between devices with their start and end apart: 4, of which 4 were waited for; matrix products, arithmetic and copies ran while one was open for 0% of the time, Pallas kernels for 0%

profile of v1, /device:TPU:0, one launch (start us, length us, event | category | flops | bytes accessed | tf_op | source)
XLA Modules:
  0.0 815.1 jit_solution(14818144485708421496)
XLA Ops:
  9.0 6.4 all-to-all-start
  16.1 8.9 %all-to-all-done = bf16[8,256,128]{2,1,0:T(8,128)(2,1)S(1)} async-done(((bf16[8,256,128]{2,1,0:T(8,128)(2,1)}), bf16[8,256,128]{2,1,0:T(8,128)(2,1)S(1)}, u32[]{:S(2)}, u32[]{:S(2)}) %all-to-all-start) | async-done | bytes 524320 | tf_op jit(solution)/shard_map/all_to_all | solution.py:28
  24.9 8.6 %gather_fusion = bf16[256,128,128]{2,1,0:T(8,128)(2,1)} fusion(bf16[16,128,128]{2,1,0:T(8,128)(2,1)S(1)} %bitcast.91, s32[1024]{0:T(1024)S(1)} %pad_clamp_fusion.1), kind=kCustom, calls=%fused_computation | custom fusion | bytes 16778240 | tf_op jit(solution)/shard_map/gather | solution.py:91
  33.5 12.8 %convolution_bitcast_fusion.5 = f32[256,128,128]{1,2,0:T(8,128)} fusion(bf16[256,128,128]{2,1,0:T(8,128)(2,1)} %gather_fusion, bf16[256,128,128]{2,1,0:T(8,128)(2,1)} %param.5), kind=kOutput, calls=%fused_computation.11 | convolution fusion | flops 1073741824 | bytes 33554432 | tf_op jit(solution)/shard_map/bij,bjk->bik/dot_general | solution.py:92
  46.4 17.5 %copy.44 = f32[256,128,128]{2,0,1:T(8,128)} copy(f32[256,128,128]{1,2,0:T(8,128)} %convolution_bitcast_fusion.5) | data formatting | bytes 33554432 | tf_op jit(solution)/shard_map/bij,bjk->bik/dot_general | solution.py:92
  63.8 9.8 %fusion.5 = f32[32,128,128]{2,0,1:T(8,128)S(1)} fusion(f32[256,128,128]{2,0,1:T(8,128)} %copy.44, s32[256]{0:T(256)S(1)} %bitcast.106), kind=kOutput, calls=%fused_computation.40 | convolution fusion | flops 1610620928 | bytes 18875392 | tf_op jit(solution)/shard_map/br,bik->rik/dot_general | solution.py:95
  76.2 6.7 all-to-all-start.1
  84.6 27.5 %all-to-all-done.1 = f32[16,256,128]{2,1,0:T(8,128)S(1)} async-done(((f32[16,256,128]{2,1,0:T(8,128)}), f32[16,256,128]{2,1,0:T(8,128)S(1)}, u32[]{:S(2)}, u32[]{:S(2)}) %all-to-all-start.1) | async-done | bytes 2097184 | tf_op jit(solution)/shard_map/all_to_all | solution.py:22
  113.5 4.9 all-to-all-start.2
  118.7 17.7 %all-to-all-done.2 = bf16[16,256,128]{2,1,0:T(8,128)(2,1)S(1)} async-done(((bf16[16,256,128]{2,1,0:T(8,128)(2,1)}), bf16[16,256,128]{2,1,0:T(8,128)(2,1)S(1)}, u32[]{:S(2)}, u32[]{:S(2)}) %all-to-all-start.2) | async-done | bytes 1048608 | tf_op jit(solution)/shard_map/all_to_all | solution.py:28
  136.4 8.6 %gather_fusion.1 = bf16[256,128,128]{2,1,0:T(8,128)(2,1)} fusion(bf16[32,128,128]{2,1,0:T(8,128)(2,1)S(1)} %bitcast.94, s32[1024]{0:T(1024)S(1)} %pad_clamp_fusion), kind=kCustom, calls=%fused_computation.1 | custom fusion | bytes 16778240 | tf_op jit(solution)/shard_map/gather | solution.py:101
  145.0 14.4 %convolution_bitcast_fusion.4 = f32[256,128,128]{1,2,0:T(8,128)} fusion(bf16[256,128,128]{2,1,0:T(8,128)(2,1)} %gather_fusion.1, bf16[256,128,128]{2,1,0:T(8,128)(2,1)} %param.5), kind=kOutput, calls=%fused_computation.10 | convolution fusion | flops 1073741824 | bytes 33554432 | tf_op jit(solution)/shard_map/bji,bjk->bik/dot_general | solution.py:102
  159.4 17.5 %copy.47 = f32[256,128,128]{2,0,1:T(8,128)} copy(f32[256,128,128]{1,2,0:T(8,128)} %convolution_bitcast_fusion.4) | data formatting | bytes 33554432 | tf_op jit(solution)/shard_map/bji,bjk->bik/dot_general | solution.py:102
  176.9 9.0 %fusion.15 = f32[16,128,128]{2,0,1:T(8,128)S(1)} fusion(f32[256,128,128]{2,0,1:T(8,128)} %copy.47, s32[256]{0:T(256)S(1)} %bitcast.103), kind=kOutput, calls=%fused_computation.49 | convolution fusion | flops 805310464 | bytes 17826816 | tf_op jit(solution)/shard_map/bc,bik->cik/dot_general | solution.py:105
  186.3 18.3 %all_to_all.60 = f32[8,256,128]{2,1,0:T(8,128)S(1)} all-to-all(f32[8,256,128]{2,1,0:T(8,128)S(1)} %bitcast.100), channel_id=1, replica_groups=mesh['row_0'=2,'row_1'=4,'col_0'=4,'col_1'=2,'col_2'=2] {'row_0','row_1'}, dimensions={0} | all-to-all | bytes 2097152 | tf_op jit(solution)/shard_map/all_to_all | solution.py:22
  205.6 4.2 all-gather.40
  209.8 4.2 all-gather.45
  218.3 7.7 all-gather.36
  226.0 7.8 all-gather.37
  233.9 5.7 all-gather.38
  241.4 8.1 all-gather.46
  249.5 8.0 all-gather.47
  257.5 5.7 all-gather.48
  265.1 7.7 all-gather.41
  272.8 7.8 all-gather.42
  280.7 5.7 all-gather.43
  289.2 13.4 %all_to_all.61 = bf16[8,256,128]{2,1,0:T(8,128)(2,1)S(1)} all-to-all(bf16[8,256,128]{2,1,0:T(8,128)(2,1)S(1)} %broadcast_in_dim.19), channel_id=1, replica_groups=mesh['row_0'=2,'row_1'=4,'col_0'=4,'col_1'=2,'col_2'=2] {'row_0','row_1'}, dimensions={0} | all-to-all | bytes 1048576 | tf_op jit(solution)/shard_map/all_to_all | solution.py:28
  302.6 8.6 %gather_fusion.2 = bf16[256,128,128]{2,1,0:T(8,128)(2,1)} fusion(bf16[16,128,128]{2,1,0:T(8,128)(2,1)S(1)} %bitcast.93, s32[1024]{0:T(1024)S(1)} %pad_clamp_fusion.1), kind=kCustom, calls=%fused_computation.2 | custom fusion | bytes 16778240 | tf_op jit(solution)/shard_map/gather | solution.py:91
  311.2 12.8 %convolution_bitcast_fusion.3 = f32[256,128,128]{1,2,0:T(8,128)} fusion(bf16[256,128,128]{2,1,0:T(8,128)(2,1)} %gather_fusion.2, bf16[256,128,128]{2,1,0:T(8,128)(2,1)} %param.5), kind=kOutput, calls=%fused_computation.9 | convolution fusion | flops 1073741824 | bytes 33554432 | tf_op jit(solution)/shard_map/bij,bjk->bik/dot_general | solution.py:92
  324.0 17.5 %copy.50 = f32[256,128,128]{2,0,1:T(8,128)} copy(f32[256,128,128]{1,2,0:T(8,128)} %convolution_bitcast_fusion.3) | data formatting | bytes 33554432 | tf_op jit(solution)/shard_map/bij,bjk->bik/dot_general | solution.py:92
  341.5 9.8 %fusion.3 = f32[32,128,128]{2,0,1:T(8,128)S(1)} fusion(f32[256,128,128]{2,0,1:T(8,128)} %copy.50, s32[256]{0:T(256)S(1)} %bitcast.107), kind=kOutput, calls=%fused_computation.39 | convolution fusion | flops 1610620928 | bytes 18875392 | tf_op jit(solution)/shard_map/br,bik->rik/dot_general | solution.py:95
  352.5 32.3 %all_to_all.62 = f32[16,256,128]{2,1,0:T(8,128)S(1)} all-to-all(f32[16,256,128]{2,1,0:T(8,128)S(1)} %bitcast.98), channel_id=1, replica_groups=mesh['row_0'=2,'row_1'=4,'col_0'=4,'col_1'=2,'col_2'=2] {'col_0','col_1'..., dimensions={0} | all-to-all | bytes 4194304 | tf_op jit(solution)/shard_map/all_to_all | solution.py:22
  385.2 20.8 %all_to_all.63 = bf16[16,256,128]{2,1,0:T(8,128)(2,1)S(1)} all-to-all(bf16[16,256,128]{2,1,0:T(8,128)(2,1)S(1)} %broadcast_in_dim.20), channel_id=1, replica_groups=mesh['row_0'=2,'row_1'=4,'col_0'=4,'col_1'=2,'col_2'=2] {'col_0','col_1'..., dimensions={0} | all-to-all | bytes 2097152 | tf_op jit(solution)/shard_map/all_to_all | solution.py:28
  406.0 8.6 %gather_fusion.3 = bf16[256,128,128]{2,1,0:T(8,128)(2,1)} fusion(bf16[32,128,128]{2,1,0:T(8,128)(2,1)S(1)} %bitcast.96, s32[1024]{0:T(1024)S(1)} %pad_clamp_fusion), kind=kCustom, calls=%fused_computation.3 | custom fusion | bytes 16778240 | tf_op jit(solution)/shard_map/gather | solution.py:101
  414.6 14.4 %convolution_bitcast_fusion.2 = f32[256,128,128]{1,2,0:T(8,128)} fusion(bf16[256,128,128]{2,1,0:T(8,128)(2,1)} %gather_fusion.3, bf16[256,128,128]{2,1,0:T(8,128)(2,1)} %param.5), kind=kOutput, calls=%fused_computation.8 | convolution fusion | flops 1073741824 | bytes 33554432 | tf_op jit(solution)/shard_map/bji,bjk->bik/dot_general | solution.py:102
  429.0 17.5 %copy.53 = f32[256,128,128]{2,0,1:T(8,128)} copy(f32[256,128,128]{1,2,0:T(8,128)} %convolution_bitcast_fusion.2) | data formatting | bytes 33554432 | tf_op jit(solution)/shard_map/bji,bjk->bik/dot_general | solution.py:102
  446.5 9.0 %fusion.13 = f32[16,128,128]{2,0,1:T(8,128)S(1)} fusion(f32[256,128,128]{2,0,1:T(8,128)} %copy.53, s32[256]{0:T(256)S(1)} %bitcast.104), kind=kOutput, calls=%fused_computation.48 | convolution fusion | flops 805310464 | bytes 17826816 | tf_op jit(solution)/shard_map/bc,bik->cik/dot_general | solution.py:105
  455.9 17.7 %all_to_all.64 = f32[8,256,128]{2,1,0:T(8,128)S(1)} all-to-all(f32[8,256,128]{2,1,0:T(8,128)S(1)} %bitcast.101), channel_id=1, replica_groups=mesh['row_0'=2,'row_1'=4,'col_0'=4,'col_1'=2,'col_2'=2] {'row_0','row_1'}, dimensions={0} | all-to-all | bytes 2097152 | tf_op jit(solution)/shard_map/all_to_all | solution.py:22
  473.6 4.2 all-gather.60
  486.3 7.7 all-gather.51
  494.1 8.0 all-gather.52
  502.1 5.7 all-gather.53
  509.6 8.1 all-gather.56
  517.7 7.9 all-gather.57
  525.6 5.7 all-gather.58
  533.1 7.7 all-gather.61
  540.9 8.0 all-gather.62
  548.9 5.7 all-gather.63
  556.5 13.3 %all_to_all.65 = bf16[8,256,128]{2,1,0:T(8,128)(2,1)S(1)} all-to-all(bf16[8,256,128]{2,1,0:T(8,128)(2,1)S(1)} %broadcast_in_dim.21), channel_id=1, replica_groups=mesh['row_0'=2,'row_1'=4,'col_0'=4,'col_1'=2,'col_2'=2] {'row_0','row_1'}, dimensions={0} | all-to-all | bytes 1048576 | tf_op jit(solution)/shard_map/all_to_all | solution.py:28
  569.8 8.6 %gather_fusion.4 = bf16[256,128,128]{2,1,0:T(8,128)(2,1)} fusion(bf16[16,128,128]{2,1,0:T(8,128)(2,1)S(1)} %bitcast.92, s32[1024]{0:T(1024)S(1)} %pad_clamp_fusion.1), kind=kCustom, calls=%fused_computation.4 | custom fusion | bytes 16778240 | tf_op jit(solution)/shard_map/gather | solution.py:91
  578.4 12.8 %convolution_bitcast_fusion.1 = f32[256,128,128]{1,2,0:T(8,128)} fusion(bf16[256,128,128]{2,1,0:T(8,128)(2,1)} %gather_fusion.4, bf16[256,128,128]{2,1,0:T(8,128)(2,1)} %param.5), kind=kOutput, calls=%fused_computation.7 | convolution fusion | flops 1073741824 | bytes 33554432 | tf_op jit(solution)/shard_map/bij,bjk->bik/dot_general | solution.py:92
  591.2 17.5 %copy.56 = f32[256,128,128]{2,0,1:T(8,128)} copy(f32[256,128,128]{1,2,0:T(8,128)} %convolution_bitcast_fusion.1) | data formatting | bytes 33554432 | tf_op jit(solution)/shard_map/bij,bjk->bik/dot_general | solution.py:92
  608.7 9.8 %fusion.1 = f32[32,128,128]{2,0,1:T(8,128)S(1)} fusion(f32[256,128,128]{2,0,1:T(8,128)} %copy.56, s32[256]{0:T(256)S(1)} %bitcast.108), kind=kOutput, calls=%fused_computation.38 | convolution fusion | flops 1610620928 | bytes 18875392 | tf_op jit(solution)/shard_map/br,bik->rik/dot_general | solution.py:95
  619.7 32.4 %all_to_all.66 = f32[16,256,128]{2,1,0:T(8,128)S(1)} all-to-all(f32[16,256,128]{2,1,0:T(8,128)S(1)} %bitcast.99), channel_id=1, replica_groups=mesh['row_0'=2,'row_1'=4,'col_0'=4,'col_1'=2,'col_2'=2] {'col_0','col_1'..., dimensions={0} | all-to-all | bytes 4194304 | tf_op jit(solution)/shard_map/all_to_all | solution.py:22
  652.5 20.8 %all_to_all.67 = bf16[16,256,128]{2,1,0:T(8,128)(2,1)S(1)} all-to-all(bf16[16,256,128]{2,1,0:T(8,128)(2,1)S(1)} %broadcast_in_dim.22), channel_id=1, replica_groups=mesh['row_0'=2,'row_1'=4,'col_0'=4,'col_1'=2,'col_2'=2] {'col_0','col_1'..., dimensions={0} | all-to-all | bytes 2097152 | tf_op jit(solution)/shard_map/all_to_all | solution.py:28
  673.3 8.6 %gather_fusion.5 = bf16[256,128,128]{2,1,0:T(8,128)(2,1)} fusion(bf16[32,128,128]{2,1,0:T(8,128)(2,1)S(1)} %bitcast.95, s32[1024]{0:T(1024)S(1)} %pad_clamp_fusion), kind=kCustom, calls=%fused_computation.5 | custom fusion | bytes 16778240 | tf_op jit(solution)/shard_map/gather | solution.py:101
  681.9 14.4 %convolution_bitcast_fusion = f32[256,128,128]{1,2,0:T(8,128)} fusion(bf16[256,128,128]{2,1,0:T(8,128)(2,1)} %gather_fusion.5, bf16[256,128,128]{2,1,0:T(8,128)(2,1)} %param.5), kind=kOutput, calls=%fused_computation.6 | convolution fusion | flops 1073741824 | bytes 33554432 | tf_op jit(solution)/shard_map/bji,bjk->bik/dot_general | solution.py:102
  696.3 17.5 %copy.59 = f32[256,128,128]{2,0,1:T(8,128)} copy(f32[256,128,128]{1,2,0:T(8,128)} %convolution_bitcast_fusion) | data formatting | bytes 33554432 | tf_op jit(solution)/shard_map/bji,bjk->bik/dot_general | solution.py:102
  713.8 9.0 %fusion.11 = f32[16,128,128]{2,0,1:T(8,128)S(1)} fusion(f32[256,128,128]{2,0,1:T(8,128)} %copy.59, s32[256]{0:T(256)S(1)} %bitcast.105), kind=kOutput, calls=%fused_computation.47 | convolution fusion | flops 805310464 | bytes 17826816 | tf_op jit(solution)/shard_map/bc,bik->cik/dot_general | solution.py:105
  723.2 17.7 %all_to_all.68 = f32[8,256,128]{2,1,0:T(8,128)S(1)} all-to-all(f32[8,256,128]{2,1,0:T(8,128)S(1)} %bitcast.102), channel_id=1, replica_groups=mesh['row_0'=2,'row_1'=4,'col_0'=4,'col_1'=2,'col_2'=2] {'row_0','row_1'}, dimensions={0} | all-to-all | bytes 2097152 | tf_op jit(solution)/shard_map/all_to_all | solution.py:22
  745.2 7.7 all-gather.66
  752.9 8.0 all-gather.67
  760.9 5.7 all-gather.68
  770.1 35.0 %all-gather.72.cloned.1.call-done = bf16[2048,256]{1,0:T(8,128)(2,1)} async-done(((bf16[256,256]{1,0:T(8,128)(2,1)}), bf16[2048,256]{1,0:T(8,128)(2,1)}) %all-gather.72.cloned.1.call-update) | async-done | bytes 1048592 | tf_op jit(solution)/shard_map/all_gather | solution.py:52
  (93 shorter events, 49.2 us)
Async XLA Ops:
  9.0 16.0 %all-to-all-start = ((bf16[8,256,128]{2,1,0:T(8,128)(2,1)}), bf16[8,256,128]{2,1,0:T(8,128)(2,1)S(1)}, u32[]{:S(2)}, u32[]{:S(2)}) async-start(bf16[8,256,128]{2,1,0:T(8,128)(2,1)} %broadcast_in_dim.17), calls=%async_computation | async-start | bytes 1048576 | tf_op jit(solution)/shard_map/all_to_all | solution.py:28
  73.6 9.3 %copy-start = (f32[4096]{0:T(1024)S(1)}, f32[4096]{0:T(1024)}, u32[]{:S(2)}) copy-start(f32[4096]{0:T(1024)} %param.7) | copy-start | bytes 49156
  73.6 9.3 %copy-start.1 = (s32[512]{0:T(512)S(1)}, s32[512]{0:T(512)}, u32[]{:S(2)}) copy-start(s32[512]{0:T(512)} %param.8) | copy-start | bytes 6148
  76.2 36.0 %all-to-all-start.1 = ((f32[16,256,128]{2,1,0:T(8,128)}), f32[16,256,128]{2,1,0:T(8,128)S(1)}, u32[]{:S(2)}, u32[]{:S(2)}) async-start(f32[16,256,128]{2,1,0:T(8,128)} %bitcast.97), calls=%async_computation.1 | async-start | bytes 4194304 | tf_op jit(solution)/shard_map/all_to_all | solution.py:22
  113.5 22.9 %all-to-all-start.2 = ((bf16[16,256,128]{2,1,0:T(8,128)(2,1)}), bf16[16,256,128]{2,1,0:T(8,128)(2,1)S(1)}, u32[]{:S(2)}, u32[]{:S(2)}) async-start(bf16[16,256,128]{2,1,0:T(8,128)(2,1)} %broadcast_in_dim.18), calls=%async_computation.2 | async-start | bytes 2097152 | tf_op jit(solution)/shard_map/all_to_all | solution.py:28
  118.4 686.7 %all-gather.72.cloned.1.call-start = ((), (), s32[]{:S(2)}) async-start(), calls=%async_computation.12 | async-start | bytes 1179648 | tf_op jit(solution)/shard_map/all_gather | solution.py:52
Sparse Core Ops, SparseCore 0:
  770.2 34.8 all-gather.71
